TPU v7x, 32 devices: a whole 2x2x4 slice. The times are simulated.
32 devices in a mesh: yz: 8 (over y, x, core), gx: 4 (over z).
Axes of the slice: x: 2, y: 2, z: 4, core: 2. Of those that a mesh axis runs over, the one named last changes fastest.
Arguments:
- state: float32 [7, 64, 64, 128], P(None, 'gx', 'yz'), may hold values from -2.5 to 2.5
- register: float32 [7, 64, 64, 128], P(None, 'gx', 'yz'), may hold values from -3 to 3
- forcing: float32 [3, 64, 64, 128], P(None, 'gx', 'yz'), may hold values from -3 to 3
- y_shift: int32 [1], replicated, may hold values from 0 to 63
Outputs:
- new_state: float32 [7, 64, 64, 128], P(None, 'gx', 'yz')
- new_register: float32 [7, 64, 64, 128], P(None, 'gx', 'yz')
All inputs are finite; a program needn't handle non-finite values.
Results may differ from a plain program's by a relative error of at most 0.000092.
Values sent between devices are 32-bit elements; how exact they have to be, the bound alone decides.
No kernel may reach another device: no remote copies, remote signals or barrier semaphores. Data moves between devices by JAX's collectives and lax.ppermute only.
A program may use at most 64 MiB of HBM per device.

v0:
```python
import functools

import jax
import jax.numpy as jnp
from jax import lax
from jax.experimental import pallas as pl
from jax.experimental.pallas import tpu as pltpu
from jax.sharding import PartitionSpec as P

LANES = 128
FIRST = ((1, 45.0), (2, -9.0), (3, 1.0))
SECOND = ((1, 270.0), (2, -27.0), (3, 2.0))
MIXED = (0, 1, 3, 4)
PLAIN = (2, 5, 6)
DEEP = (0, 2, 3, 5)
SHEAR_Z = (1, 2, 4, 5)
ROW = 8
LOW = 10**9
EARLY = 4
TALL = 24
VMEM = 32 * 1024 * 1024


def z_weights():
    source = lax.broadcasted_iota(jnp.int32, (LANES, LANES), 0)
    cell = lax.broadcasted_iota(jnp.int32, (LANES, LANES), 1)
    ahead = (source - cell) & (LANES - 1)
    first = jnp.zeros((LANES, LANES), jnp.float32)
    second = jnp.where(ahead == 0, -490.0, 0.0)
    for step, weight in FIRST:
        first = jnp.where(ahead == step, weight, jnp.where(ahead == LANES - step, -weight, first))
    for step, weight in SECOND:
        second = jnp.where((ahead == step) | (ahead == LANES - step), weight, second)
    one = jnp.concatenate([first, second], axis=1)
    return jnp.concatenate([one, one]).astype(jnp.bfloat16)


def along_z(value, weights):
    upper = value.astype(jnp.bfloat16)
    rest = (value - upper.astype(jnp.float32)).astype(jnp.bfloat16)
    return jnp.dot(
        jnp.concatenate([upper, rest], axis=1), weights, preferred_element_type=jnp.float32
    )


def first_diff(part):
    return (
        0.75 * (part(1) - part(-1))
        - 0.15 * (part(2) - part(-2))
        + (1.0 / 60.0) * (part(3) - part(-3))
    )


def second_diff(part):
    return (
        (-490.0 / 180.0) * part(0)
        + 1.5 * (part(1) + part(-1))
        - 0.15 * (part(2) + part(-2))
        + (1.0 / 90.0) * (part(3) + part(-3))
    )


def x_terms(planes_of, deep_of):
    grad = [first_diff(planes_of(field)) for field in range(7)]
    viscous = [
        (4.0 / 3.0) * second_diff(planes_of(0)) + (1.0 / 3.0) * first_diff(deep_of(2)),
        second_diff(planes_of(1)),
        second_diff(planes_of(2)) + (1.0 / 3.0) * first_diff(deep_of(0)),
    ]
    current = [
        first_diff(deep_of(5)),
        -second_diff(planes_of(4)),
        first_diff(deep_of(3)) - second_diff(planes_of(5)),
    ]
    return grad + viscous + current


def xy_terms(parts, side_of):
    parts = list(parts)
    parts[7] = parts[7] + (1.0 / 3.0) * first_diff(side_of(1))
    parts[8] = parts[8] + (1.0 / 3.0) * first_diff(side_of(0))
    parts[10] = parts[10] + first_diff(side_of(4))
    parts[11] = parts[11] + first_diff(side_of(3))
    return parts


def rates_of(center, force, index, inv_width, grads, viscous, curr):
    velx, vely, velz, potx, poty, potz, logr = center
    grad_x, grad_y, grad_z = grads
    field_x = grad_y[5] - grad_z[4]
    field_y = grad_z[3] - grad_x[5]
    field_z = grad_x[4] - grad_y[3] + 0.5
    lorentz = (
        curr[1] * field_z - curr[2] * field_y,
        curr[2] * field_x - curr[0] * field_z,
        curr[0] * field_y - curr[1] * field_x,
    )
    emf = (
        vely * field_z - velz * field_y,
        velz * field_x - velx * field_z,
        velx * field_y - vely * field_x,
    )
    inv_rho = jnp.exp(-logr)
    flow = -1.5 * ((index.astype(jnp.float32) + 0.5) * inv_width - 0.5)
    shear_rate = -1.5 * inv_width
    carried = vely + flow
    divu = grad_x[0] + grad_y[1] + grad_z[2]

    def advect(comp):
        return velx * grad_x[comp] + carried * grad_y[comp] + velz * grad_z[comp]

    rates = []
    for comp in range(3):
        total = (-2.0 / 3.0) * divu * grads[comp][6]
        for col in range(3):
            total = total + (grads[col][comp] + grads[comp][col]) * grads[col][6]
        rate = lorentz[comp] * inv_rho - advect(comp) - grads[comp][6] + force[comp]
        rate = rate + 0.05 * (viscous[comp] + total)
        if comp == 0:
            rate = rate + vely
        if comp == 1:
            rate = rate - (1.0 + shear_rate) * velx
        rates.append(rate)
    for comp in range(3):
        rate = emf[comp] - flow * grad_y[3 + comp] - 0.05 * curr[comp]
        if comp == 0:
            rate = rate - shear_rate * poty
        rates.append(rate)
    rates.append(-advect(6) - divu)
    return rates


def face_kernel(cells_x, state, up, down):
    up[...] = state[:, cells_x - 3 :]
    down[...] = state[:, :3]


def low_kernel(x_low, after, low):
    low[...] = x_low[...]


def row_kernel(cells_x, cells_y, state, y_near, y_far):
    y_odd = lax.axis_index("yz") % 2

    def rows(first, then):
        for field in range(7):
            for plane in range(cells_x):
                at = 3 * (field * cells_x + plane)
                first[at : at + 3] = state[field, plane, cells_y - 3 :]
                then[at : at + 3] = state[field, plane, :3]

    pl.when(y_odd == 0)(functools.partial(rows, y_near, y_far))
    pl.when(y_odd == 1)(functools.partial(rows, y_far, y_near))


def weight_kernel(weights):
    weights[...] = z_weights()


def own_z_kernel(cells_x, state, weights, forcing, dz, dzz, force, sem):
    copy = pltpu.make_async_copy(forcing, force, sem)
    copy.start()
    got = along_z(state[...].reshape(7 * cells_x * 8, LANES), weights[...])
    dz[...] = (got[:, :LANES] * (1.0 / 60.0)).reshape(7, cells_x, 8, LANES)
    dzz[...] = (got[: 5 * cells_x * 8, LANES:] * (1.0 / 180.0)).reshape(5, cells_x, 8, LANES)
    copy.wait()


def across_kernel(cells_x, state, dz, after, x_parts):
    def plane_step(plane):
        terms = x_terms(
            lambda field: lambda step: state[field, plane + step],
            lambda field: lambda step: dz[field, plane + step],
        )
        for number, term in enumerate(terms):
            x_parts[number, plane - 3] = term

    in_pairs(3, cells_x - 3, plane_step)


def side_kernel(
    cells_x, state, weights, y_far, y_near, dz, dzz, after, side_terms, block, z_block
):
    own = slice(ROW, ROW + 8)
    y_odd = lax.axis_index("yz") % 2
    block[:, :, own] = state[...]
    for number, field in enumerate(SHEAR_Z):
        z_block[number, :, own] = dz[field]
    count = 3 * cells_x
    got = along_z(
        jnp.concatenate(
            [rows[field * count : (field + 1) * count] for rows in (y_near, y_far) for field in SHEAR_Z]
        ),
        weights[:, :LANES],
    ) * (1.0 / 60.0)

    def ghosts(target, rows, begin):
        for field in range(7):
            for plane in range(cells_x):
                at = 3 * (field * cells_x + plane)
                block[field, plane, target : target + 3] = rows[at : at + 3]
        for number in range(4):
            for plane in range(cells_x):
                at = begin + 3 * (number * cells_x + plane)
                z_block[number, plane, target : target + 3] = got[at : at + 3]

    @pl.when(y_odd == 0)
    def _():
        ghosts(ROW + 8, y_near, 0)
        ghosts(ROW - 3, y_far, 4 * count)

    @pl.when(y_odd == 1)
    def _():
        ghosts(ROW - 3, y_near, 0)
        ghosts(ROW + 8, y_far, 4 * count)

    def yz_step(plane):
        def rows_of(field):
            return lambda step: block[field, plane, ROW + step : ROW + 8 + step]

        def z_rows_of(number):
            return lambda step: z_block[number, plane, ROW + step : ROW + 8 + step]

        grad = [first_diff(rows_of(field)) for field in range(7)]
        cross = [first_diff(z_rows_of(number)) for number in range(4)]
        terms = grad + [
            second_diff(rows_of(0)) + dzz[0, plane],
            (4.0 / 3.0) * second_diff(rows_of(1)) + dzz[1, plane] + (1.0 / 3.0) * cross[1],
            second_diff(rows_of(2)) + (4.0 / 3.0) * dzz[2, plane] + (1.0 / 3.0) * cross[0],
            -(second_diff(rows_of(3)) + dzz[3, plane]),
            cross[3] - dzz[4, plane],
            cross[2] - second_diff(rows_of(5)),
        ]
        for number, term in enumerate(terms):
            side_terms[number, plane] = term

    in_pairs(0, cells_x, yz_step)


def in_pairs(begin, end, step):
    def two(number, carry):
        step(begin + 2 * number)
        step(begin + 2 * number + 1)
        return carry

    lax.fori_loop(0, (end - begin) // 2, two, 0)


def corner_kernel(slabs_x, low, x_high, faces, far, near):
    where_x = lax.axis_index("gx")
    y_odd = lax.axis_index("yz") % 2
    faces[0] = low[...]
    faces[1] = x_high[...]

    def fill(to_next, to_last):
        for side in range(2):
            for number, field in enumerate(MIXED):
                for plane in range(3):
                    at = 3 * (3 * (4 * side + number) + plane)
                    to_next[at : at + 3] = faces[side, field, plane, 5:8]
                    to_last[at : at + 3] = faces[side, field, plane, 0:3]

        def sheared(side):
            for number, field in enumerate(MIXED + PLAIN):
                for plane in range(3):
                    at = 72 + 4 * (3 * number + plane)
                    row = 1 if field in MIXED else 4
                    to_next[at : at + 4] = faces[side, field, plane, row : row + 4]
                    row = 3 if field in MIXED else 0
                    to_last[at : at + 4] = faces[side, field, plane, row : row + 4]

        pl.when(where_x == 0)(functools.partial(sheared, 0))
        pl.when(where_x == slabs_x - 1)(functools.partial(sheared, 1))

    pl.when(y_odd == 0)(functools.partial(fill, near, far))
    pl.when(y_odd == 1)(functools.partial(fill, far, near))


def copies_out(parts, finals, begin, count, sems, base):
    return [
        pltpu.make_async_copy(
            part.at[field], final.at[field, pl.ds(begin, count)], sems.at[base + 7 * which + field]
        )
        for which, (part, final) in enumerate(zip(parts, finals))
        for field in range(7)
    ]


def finish(inv_width, index, center, force, old, x_parts, side, grad_z):
    rates = rates_of(
        center,
        force,
        index,
        inv_width,
        (x_parts[:7], side[:7], grad_z),
        [x_parts[7 + comp] + side[7 + comp] for comp in range(3)],
        [x_parts[10 + comp] + side[10 + comp] for comp in range(3)],
    )
    fresh = [(-5.0 / 9.0) * old[field] + 0.15 * rates[field] for field in range(7)]
    return [center[field] + (15.0 / 16.0) * fresh[field] for field in range(7)], fresh


def inner_kernel(
    cells_x, inv_width,
    state, register, forcing, dz, x_parts, side_terms,
    new_state, new_register, late_state, late_register,
    fresh_state, fresh_register, sems,
):
    first = lax.axis_index("gx") * cells_x
    early = EARLY

    def step_into(states_out, registers_out, begin):
        def plane_step(plane):
            states, registers = finish(
                inv_width,
                first + plane,
                [state[field, plane] for field in range(7)],
                [forcing[comp, plane] for comp in range(3)],
                [register[field, plane] for field in range(7)],
                xy_terms(
                    [x_parts[number, plane - 3] for number in range(13)],
                    lambda field: lambda step: side_terms[field, plane + step],
                ),
                [side_terms[number, plane] for number in range(13)],
                [dz[field, plane] for field in range(7)],
            )
            for field in range(7):
                registers_out[field, plane - begin] = registers[field]
                states_out[field, plane - begin] = states[field]

        return plane_step

    in_pairs(3, 3 + early, step_into(fresh_state, fresh_register, 3))
    copies = copies_out((fresh_state, fresh_register), (new_state, new_register), 3, early, sems, 0)
    for copy in copies:
        copy.start()
    in_pairs(3 + early, cells_x - 3, step_into(late_state, late_register, 3 + early))
    for copy in copies:
        copy.wait()


def edge_kernel(
    cells_x, slabs_x, inv_width,
    lean_tile, state, register, forcing, weights, dz, side_terms,
    planes, far, near, late_state, late_register, kept_state, kept_register,
    new_state, new_register,
    ghost, fields, deep, slope, fresh_state, fresh_register, sems,
):
    finals = (new_state, new_register)
    late = copies_out((late_state, late_register), finals, 3 + EARLY, cells_x - 6 - EARLY, sems, 0)
    for copy in late:
        copy.start()
    where_x = lax.axis_index("gx")
    y_odd = lax.axis_index("yz") % 2
    first = where_x * cells_x
    lean = lean_tile[...][0, 0]
    at_low, at_high = where_x == 0, where_x == slabs_x - 1
    for field in range(7):
        fields[0, field, 3:9] = state[field, 0:6]
        fields[1, field, 0:6] = state[field, cells_x - 6 :]
    for number, field in enumerate(DEEP):
        deep[0, number, 3:9] = dz[field, 0:6]
        deep[1, number, 0:6] = dz[field, cells_x - 6 :]
    for number, field in enumerate(MIXED):
        slope[0, number, 3:9] = side_terms[field, 0:6]
        slope[1, number, 0:6] = side_terms[field, cells_x - 6 :]
    for side in range(2):
        for field in range(7):
            for plane in range(3):
                ghost[side, field, plane, 16:24] = planes[side, field, plane]

    def put(from_last, from_next):
        for side in range(2):
            for number, field in enumerate(MIXED):
                for plane in range(3):
                    at = 3 * (3 * (4 * side + number) + plane)
                    ghost[side, field, plane, 13:16] = from_last[at : at + 3]
                    ghost[side, field, plane, 24:27] = from_next[at : at + 3]

        def sheared(side):
            for number, field in enumerate(MIXED + PLAIN):
                for plane in range(3):
                    at = 72 + 4 * (3 * number + plane)
                    row = 9 if field in MIXED else 12
                    ghost[side, field, plane, row : row + 4] = from_last[at : at + 4]
                    row = 27 if field in MIXED else 24
                    ghost[side, field, plane, row : row + 4] = from_next[at : at + 4]

        pl.when(at_low)(functools.partial(sheared, 0))
        pl.when(at_high)(functools.partial(sheared, 1))

    pl.when(y_odd == 0)(functools.partial(put, far, near))
    pl.when(y_odd == 1)(functools.partial(put, near, far))
    for side, shift in enumerate((jnp.where(at_low, lean, 0), jnp.where(at_high, -lean, 0))):
        for field in range(7):
            for plane in range(3):
                low = ghost[side, field, plane, pl.ds(shift + 13, 8)]
                if field in MIXED:
                    high = ghost[side, field, plane, pl.ds(shift + 21, 8)]
                    ghost[side, field, plane, 0:8] = low
                    ghost[side, field, plane, 8:16] = high
                    fields[side, field, plane + 6 * side] = ghost[side, field, plane, 3:11]
                else:
                    fields[side, field, plane + 6 * side] = ghost[side, field, plane, pl.ds(shift + 16, 8)]
    got = along_z(
        jnp.concatenate(
            [
                fields[side, field, 6 * side : 6 * side + 3].reshape(24, LANES)
                for side in range(2)
                for field in DEEP
            ]
        ),
        weights[:, :LANES],
    ) * (1.0 / 60.0)
    for side in range(2):
        for number in range(4):
            at = 24 * (4 * side + number)
            deep[side, number, 6 * side : 6 * side + 3] = got[at : at + 24].reshape(3, 8, LANES)
        for number, field in enumerate(MIXED):
            for plane in range(3):
                slope[side, number, plane + 6 * side] = first_diff(
                    lambda step: ghost[side, field, plane, 3 + step : 11 + step]
                )

    def copies_of(side):
        parts = (fresh_state.at[side], fresh_register.at[side])
        return copies_out(parts, finals, side * (cells_x - 3), 3, sems, 14 * (side + 1))

    for side in range(2):
        for local in range(3):
            plane = side * (cells_x - 3) + local
            states, registers = finish(
                inv_width,
                first + plane,
                [state[field, plane] for field in range(7)],
                [forcing[comp, plane] for comp in range(3)],
                [register[field, plane] for field in range(7)],
                xy_terms(
                    x_terms(
                        lambda field: lambda step: fields[side, field, local + 3 + step],
                        lambda field: lambda step: deep[side, DEEP.index(field), local + 3 + step],
                    ),
                    lambda field: lambda step: slope[side, MIXED.index(field), local + 3 + step],
                ),
                [side_terms[number, plane] for number in range(13)],
                [dz[field, plane] for field in range(7)],
            )
            for field in range(7):
                fresh_register[side, field, local] = registers[field]
                fresh_state[side, field, local] = states[field]
        for copy in copies_of(side):
            copy.start()
    for copy in late + copies_of(0) + copies_of(1):
        copy.wait()


def per_device(slabs_x, slabs_y, state, register, forcing, y_shift):
    cells_x, cells_y = state.shape[1], state.shape[2]
    total_x, total_y = cells_x * slabs_x, cells_y * slabs_y
    offset = y_shift[0]
    steps = (offset + cells_y // 2) // cells_y

    def shape(*dims):
        return jax.ShapeDtypeStruct(dims, jnp.float32)

    vmem = pl.BlockSpec(memory_space=pltpu.VMEM)
    anyspace = pl.BlockSpec(memory_space=pl.ANY)
    params = pltpu.CompilerParams(vmem_limit_bytes=VMEM)
    lean = lax.optimization_barrier(jnp.full((8, LANES), offset - steps * cells_y, jnp.int32))

    digit = min(slabs_y, 8)

    def place(slab, along):
        return along % slabs_y * slabs_x + slab

    def send(value, pairs):
        return lax.ppermute(value, ("yz", "gx"), pairs)

    def both(pairs):
        return pairs + [(b, a) for a, b in pairs]

    def y_pairs(odd):
        return both(
            [(place(slab, j), place(slab, j + 1)) for slab in range(slabs_x) for j in range(odd, slabs_y, 2)]
        )

    def upward(by):
        pairs = [(place(slab, j), place(slab + 1, j)) for slab in range(last) for j in range(slabs_y)]
        return pairs + [(place(last, j + by), place(0, j)) for j in range(slabs_y)]

    def downward(by):
        pairs = [(place(slab + 1, j), place(slab, j)) for slab in range(last) for j in range(slabs_y)]
        return pairs + [(place(0, j - by), place(last, j)) for j in range(slabs_y)]

    last = slabs_x - 1

    def cost(flops, moved=10**6):
        return pl.CostEstimate(flops=flops, bytes_accessed=moved, transcendentals=0)

    weights = pl.pallas_call(
        weight_kernel,
        out_shape=jax.ShapeDtypeStruct((2 * LANES, 2 * LANES), jnp.bfloat16),
        out_specs=vmem,
        compiler_params=params,
        cost_estimate=cost(2 * 10**8),
    )()

    def in_hbm(value):
        return pltpu.with_memory_space_constraint(value, pltpu.HBM)

    def faces_of(state):
        return pl.pallas_call(
            functools.partial(face_kernel, cells_x),
            out_shape=[shape(7, 3, cells_y, LANES)] * 2,
            in_specs=[vmem],
            out_specs=[vmem] * 2,
            compiler_params=params,
        )(state)

    up = down = None
    if slabs_y > digit:
        up, down = faces_of(state)
        where_x = lax.axis_index("gx")
        at_low, at_high = where_x == 0, where_x == last
        groups = steps // digit
        amount = jnp.where(at_high, groups, slabs_y // digit - groups) % (slabs_y // digit)
        across = jnp.where(at_high, up, down)
        hop = 1
        while hop < slabs_y // digit:
            pairs = [(i, (i - hop * digit) % slabs_y) for i in range(slabs_y)]
            moved = lax.ppermute(across, "yz", pairs)
            across = jnp.where((amount // hop) % 2 == 1, moved, across)
            hop *= 2
        up = jnp.where(at_high, across, up)
        down = jnp.where(at_low, across, down)

    def exchange(by, operands):
        up, down, state, register, forcing, weights, lean = operands
        plane = state.shape[1:]
        if up is None:
            up, down = faces_of(state)
        x_low = send(up, upward(by))
        x_high = send(down, downward(by))
        y_near, y_far = pl.pallas_call(
            functools.partial(row_kernel, cells_x, cells_y),
            out_shape=[shape(21 * cells_x, LANES), shape(21 * cells_x, LANES)],
            in_specs=[vmem],
            out_specs=[vmem] * 2,
            compiler_params=params,
        )(state)
        y_far = send(y_far, y_pairs(1))
        y_near = send(y_near, y_pairs(0))
        hbm = pl.BlockSpec(memory_space=pltpu.HBM)
        dz, dzz, force = pl.pallas_call(
            functools.partial(own_z_kernel, cells_x),
            out_shape=[shape(7, *plane), shape(5, *plane), shape(*forcing.shape)],
            in_specs=[vmem] * 2 + [hbm],
            out_specs=[vmem] * 3,
            scratch_shapes=[pltpu.SemaphoreType.DMA],
            compiler_params=params,
            cost_estimate=cost(10**8),
        )(state, weights, forcing)
        low = pl.pallas_call(
            low_kernel,
            out_shape=shape(*up.shape),
            in_specs=[vmem, anyspace],
            out_specs=vmem,
            compiler_params=params,
            cost_estimate=cost(LOW, 1),
        )(x_low, dz)
        faces, far, near = pl.pallas_call(
            functools.partial(corner_kernel, slabs_x),
            out_shape=[shape(2, *up.shape), shape(160, LANES), shape(160, LANES)],
            in_specs=[vmem] * 2,
            out_specs=[vmem] * 3,
            compiler_params=params,
            cost_estimate=cost(1, 1),
        )(low, x_high)
        far = send(far, y_pairs(1))
        near = send(near, y_pairs(0))
        x_parts = pl.pallas_call(
            functools.partial(across_kernel, cells_x),
            out_shape=shape(13, cells_x - 6, *plane[1:]),
            in_specs=[vmem] * 2 + [anyspace],
            out_specs=vmem,
            compiler_params=params,
            cost_estimate=cost(1, 1),
        )(state, dz, faces)
        side_terms = pl.pallas_call(
            functools.partial(side_kernel, cells_x),
            out_shape=shape(13, *plane),
            in_specs=[vmem] * 6 + [anyspace],
            out_specs=vmem,
            scratch_shapes=[
                pltpu.VMEM((7, cells_x, TALL, LANES), jnp.float32),
                pltpu.VMEM((4, cells_x, TALL, LANES), jnp.float32),
            ],
            compiler_params=params,
            cost_estimate=cost(2 * 10**8),
        )(state, weights, y_far, y_near, dz, dzz, x_parts)
        early, late = EARLY, cells_x - 6 - EARLY
        new_state, new_register, late_state, late_register = pl.pallas_call(
            functools.partial(inner_kernel, cells_x, 1.0 / total_x),
            out_shape=[shape(*state.shape)] * 2 + [shape(7, late, *plane[1:])] * 2,
            in_specs=[vmem] * 6,
            out_specs=[anyspace] * 2 + [vmem] * 2,
            scratch_shapes=[
                pltpu.VMEM((7, early, *plane[1:]), jnp.float32),
                pltpu.VMEM((7, early, *plane[1:]), jnp.float32),
                pltpu.SemaphoreType.DMA((14,)),
            ],
            compiler_params=params,
            cost_estimate=cost(2 * 10**8),
        )(state, register, force, dz, x_parts, side_terms)
        return pl.pallas_call(
            functools.partial(edge_kernel, cells_x, slabs_x, 1.0 / total_x),
            out_shape=[shape(*state.shape)] * 2,
            in_specs=[vmem] * 12 + [anyspace] * 2,
            out_specs=[anyspace] * 2,
            input_output_aliases={12: 0, 13: 1},
            scratch_shapes=[
                pltpu.VMEM((2, 7, 3, 40, LANES), jnp.float32),
                pltpu.VMEM((2, 7, 9, 8, LANES), jnp.float32),
                pltpu.VMEM((2, 4, 9, 8, LANES), jnp.float32),
                pltpu.VMEM((2, 4, 9, 8, LANES), jnp.float32),
                pltpu.VMEM((2, 7, 3, 8, LANES), jnp.float32),
                pltpu.VMEM((2, 7, 3, 8, LANES), jnp.float32),
                pltpu.SemaphoreType.DMA((42,)),
            ],
            compiler_params=params,
        )(
            lean, state, register, force, weights, dz, side_terms,
            faces, far, near, late_state, late_register, new_state, new_register,
        )

    return lax.switch(
        steps % digit,
        [functools.partial(exchange, by) for by in range(digit)],
        (up, down, state, register, in_hbm(forcing), weights, lean),
    )


def solution(mesh):
    spec = P(None, "gx", "yz", None)
    return jax.shard_map(
        functools.partial(per_device, mesh.shape["gx"], mesh.shape["yz"]),
        mesh=mesh,
        in_specs=(spec, spec, spec, P()),
        out_specs=(spec, spec),
        check_vma=False,
    )
```

profile of v0, /device:TPU:0, one launch (start us, length us, event | category | flops | bytes accessed | tf_op | source)
XLA Modules:
  0.0 20.0 jit_solution(13560331276822397156)
XLA Ops:
  0.6 0.0 copy-start
  1.4 0.1 shard_map.99
  1.4 0.2 %copy-done = f32[7,16,8,128]{3,2,1,0:T(8,128)S(1)} copy-done((f32[7,16,8,128]{3,2,1,0:T(8,128)S(1)}, f32[7,16,8,128]{3,2,1,0:T(8,128)}, u32[]{:S(2)}) %copy-start) | copy-done | bytes 458776
  1.7 18.1 %conditional.1 = ((f32[7,16,8,128]{3,2,1,0:T(8,128)}, f32[7,16,8,128]{3,2,1,0:T(8,128)})) conditional(s32[]{:T(128)} %clamp.3, (f32[7,16,8,128]{3,2,1,0:T(8,128)S(1)}, bf16[256,256]{1,0:T(8,128)(2,1)S(1)}, f32[3,16,8,128]{3,2,1,0:T(8,128)}, f32[7,16,8,128]{3,2,1,0:T(8,128)}, s32[8,128]{1,0:T(8,128)S(1)}) %tuple.64, ...), branch_computations={%region_0.1_spmd, %region_1.2_spmd, %region_2.3_spmd, %region_3.4_... | conditional | flops 1500000000 | bytes 7555031 | solution.py:636
  1.7 3.1 %collective-permute-start.38 = (f32[7,3,8,128]{3,2,1,0:T(8,128)S(1)}, f32[7,3,8,128]{3,2,1,0:T(8,128)S(1)}, u32[]{:S(2)}, u32[]{:S(2)}) collective-permute-start(f32[7,3,8,128]{3,2,1,0:T(8,128)S(1)} %get-tuple-element.204), channel_id=1, source_target_pairs={{0,1},{4,5},{8,9},{12,13},{16,17},{20,21},{24,25},{28,29},{1,2},{5... | collective-permute-start | bytes 258056 | tf_op jit(solution)/shard_map/cond/branch_6_fun/ppermute | solution.py:477
  4.8 0.1 branch_6_fun.10
  4.9 1.7 %collective-permute-start.36 = (f32[336,128]{1,0:T(8,128)S(1)}, f32[336,128]{1,0:T(8,128)S(1)}, u32[]{:S(2)}, u32[]{:S(2)}) collective-permute-start(f32[336,128]{1,0:T(8,128)S(1)} %get-tuple-element.201), channel_id=1, source_target_pairs={{4,8},{12,16},{20,24},{28,0},{5,9},{13,17},{21,25},{29,1},{6,10},{... | collective-permute-start | bytes 516104 | tf_op jit(solution)/shard_map/cond/branch_6_fun/ppermute | solution.py:477
  6.6 0.0 collective-permute-start.37
  6.6 4.0 %collective-permute-start.39 = (f32[7,3,8,128]{3,2,1,0:T(8,128)S(1)}, f32[7,3,8,128]{3,2,1,0:T(8,128)S(1)}, u32[]{:S(2)}, u32[]{:S(2)}) collective-permute-start(f32[7,3,8,128]{3,2,1,0:T(8,128)S(1)} %get-tuple-element.205), channel_id=1, source_target_pairs={{1,0},{5,4},{9,8},{13,12},{17,16},{21,20},{25,24},{29,28},{2,1},{6... | collective-permute-start | bytes 258056 | tf_op jit(solution)/shard_map/cond/branch_6_fun/ppermute | solution.py:477
  10.6 0.9 %branch_6_fun.9 = (f32[7,16,8,128]{3,2,1,0:T(8,128)S(1)}, f32[5,16,8,128]{3,2,1,0:T(8,128)S(1)}, f32[3,16,8,128]{3,2,1,0:T(8,128)S(1)}) custom-call(f32[7,16,8,128]{3,2,1,0:T(8,128)S(1)} %get-tuple-element.282.state, bf16[256,256]{1,0:T(8,128)(2,1)S(1)} %get-tuple-element.197.weights, f32[3,16,8,128]{3,2,1,0:T(8,128)} %get-tuple-element.290.forcing), custom_call_target="tpu_custom_call" | custom-call | flops 100000000 | bytes 1000000 | tf_op jit(solution)/shard_map/cond/branch_6_fun/pallas_call | solution.py:554
  11.6 0.0 collective-permute-done.38.x_low
  11.6 1.1 %collective-permute-done.39.x_high = f32[7,3,8,128]{3,2,1,0:T(8,128)S(1)} collective-permute-done((f32[7,3,8,128]{3,2,1,0:T(8,128)S(1)}, f32[7,3,8,128]{3,2,1,0:T(8,128)S(1)}, u32[]{:S(2)}, u32[]{:S(2)}) %collective-permute-start.39) | collective-permute-done | bytes 86048 | tf_op jit(solution)/shard_map/cond/branch_6_fun/ppermute | solution.py:477
  12.7 0.1 branch_6_fun.13
  12.8 0.6 %collective-permute-start.40 = (f32[160,128]{1,0:T(8,128)S(1)}, f32[160,128]{1,0:T(8,128)S(1)}, u32[]{:S(2)}, u32[]{:S(2)}) collective-permute-start(f32[160,128]{1,0:T(8,128)S(1)} %get-tuple-element.207), channel_id=1, source_target_pairs={{4,8},{12,16},{20,24},{28,0},{5,9},{13,17},{21,25},{29,1},{6,10},{... | collective-permute-start | bytes 245768 | tf_op jit(solution)/shard_map/cond/branch_6_fun/ppermute | solution.py:477
  13.4 0.4 %collective-permute-start.41 = (f32[160,128]{1,0:T(8,128)S(1)}, f32[160,128]{1,0:T(8,128)S(1)}, u32[]{:S(2)}, u32[]{:S(2)}) collective-permute-start(f32[160,128]{1,0:T(8,128)S(1)} %get-tuple-element.208), channel_id=1, source_target_pairs={{0,4},{8,12},{16,20},{24,28},{1,5},{9,13},{17,21},{25,29},{2,6},{1... | collective-permute-start | bytes 245768 | tf_op jit(solution)/shard_map/cond/branch_6_fun/ppermute | solution.py:477
  13.8 0.2 %branch_6_fun.14.after.x_parts = f32[13,10,8,128]{3,2,1,0:T(8,128)S(1)} custom-call(f32[7,16,8,128]{3,2,1,0:T(8,128)S(1)} %get-tuple-element.282.state, f32[7,16,8,128]{3,2,1,0:T(8,128)S(1)} %get-tuple-element.200.after.dz, f32[2,7,3,8,128]{4,3,2,1,0:T(8,128)S(1)} %get-tuple-element.206.after.planes), custom_call_target="tpu_custom_call" | custom-call | flops 1 | bytes 1 | tf_op jit(solution)/shard_map/cond/branch_6_fun/pallas_call | solution.py:581
  14.0 0.2 %collective-permute-done.36.y_far = f32[336,128]{1,0:T(8,128)S(1)} collective-permute-done((f32[336,128]{1,0:T(8,128)S(1)}, f32[336,128]{1,0:T(8,128)S(1)}, u32[]{:S(2)}, u32[]{:S(2)}) %collective-permute-start.36) | collective-permute-done | bytes 172064 | tf_op jit(solution)/shard_map/cond/branch_6_fun/ppermute | solution.py:477
  14.3 0.0 collective-permute-done.37.y_near
  14.3 0.0 copy-start.7
  14.3 1.0 %branch_6_fun.15.side_terms = f32[13,16,8,128]{3,2,1,0:T(8,128)S(1)} custom-call(f32[7,16,8,128]{3,2,1,0:T(8,128)S(1)} %get-tuple-element.282.state, bf16[256,256]{1,0:T(8,128)(2,1)S(1)} %get-tuple-element.197.weights, f32[336,128]{1,0:T(8,128)S(1)} %collective-permute-done.36.y_far, f32[336,128]{1,0:T(8,128)S(1)} %collective-permute-done.37.y_near, ...), custom_call_target="tpu_custom_call" | custom-call | flops 200000000 | bytes 1000000 | tf_op jit(solution)/shard_map/cond/branch_6_fun/pallas_call | solution.py:589
  15.3 0.0 copy-done.7
  15.3 0.9 %branch_6_fun.16 = (f32[7,16,8,128]{3,2,1,0:T(8,128)}, f32[7,16,8,128]{3,2,1,0:T(8,128)}, f32[7,6,8,128]{3,2,1,0:T(8,128)S(1)}, f32[7,6,8,128]{3,2,1,0:T(8,128)S(1)}) custom-call(f32[7,16,8,128]{3,2,1,0:T(8,128)S(1)} %get-tuple-element.282.state, f32[7,16,8,128]{3,2,1,0:T(8,128)S(1)} %copy-done.7, f32[3,16,8,128]{3,2,1,0:T(8,128)S(1)} %get-tuple-element.199.forcing, ...), custom_call_target="tpu_custom_call" | custom-call | flops 200000000 | bytes 1000000 | tf_op jit(solution)/shard_map/cond/branch_6_fun/pallas_call | solution.py:602
  16.2 1.7 %collective-permute-done.40.far = f32[160,128]{1,0:T(8,128)S(1)} collective-permute-done((f32[160,128]{1,0:T(8,128)S(1)}, f32[160,128]{1,0:T(8,128)S(1)}, u32[]{:S(2)}, u32[]{:S(2)}) %collective-permute-start.40) | collective-permute-done | bytes 81952 | tf_op jit(solution)/shard_map/cond/branch_6_fun/ppermute | solution.py:477
  17.9 0.0 collective-permute-done.41.near
  17.9 1.6 %branch_6_fun.17 = (f32[7,16,8,128]{3,2,1,0:T(8,128)}, f32[7,16,8,128]{3,2,1,0:T(8,128)}) custom-call(s32[8,128]{1,0:T(8,128)S(1)} %get-tuple-element.194.lean_tile, f32[7,16,8,128]{3,2,1,0:T(8,128)S(1)} %get-tuple-element.282.state, f32[7,16,8,128]{3,2,1,0:T(8,128)S(1)} %copy-done.7, ...), custom_call_target="tpu_custom_call", output_to_operand_aliasing={{0}: (12, {}), {1}: (13, {})} | custom-call | tf_op jit(solution)/shard_map/cond/branch_6_fun/pallas_call | solution.py:615
  (3 shorter events, 0.0 us)
Async XLA Ops:
  0.6 1.0 %copy-start = (f32[7,16,8,128]{3,2,1,0:T(8,128)S(1)}, f32[7,16,8,128]{3,2,1,0:T(8,128)}, u32[]{:S(2)}) copy-start(f32[7,16,8,128]{3,2,1,0:T(8,128)} %param.12) | copy-start | bytes 1376260
  1.7 9.8 %collective-permute-start.38 = (f32[7,3,8,128]{3,2,1,0:T(8,128)S(1)}, f32[7,3,8,128]{3,2,1,0:T(8,128)S(1)}, u32[]{:S(2)}, u32[]{:S(2)}) collective-permute-start(f32[7,3,8,128]{3,2,1,0:T(8,128)S(1)} %get-tuple-element.204), channel_id=1, source_target_pairs={{0,1},{4,5},{8,9},{12,13},{16,17},{20,21},{24,25},{28,29},{1,2},{5... | collective-permute-start | bytes 258056 | tf_op jit(solution)/shard_map/cond/branch_6_fun/ppermute | solution.py:477
  4.9 9.4 %collective-permute-start.36 = (f32[336,128]{1,0:T(8,128)S(1)}, f32[336,128]{1,0:T(8,128)S(1)}, u32[]{:S(2)}, u32[]{:S(2)}) collective-permute-start(f32[336,128]{1,0:T(8,128)S(1)} %get-tuple-element.201), channel_id=1, source_target_pairs={{4,8},{12,16},{20,24},{28,0},{5,9},{13,17},{21,25},{29,1},{6,10},{... | collective-permute-start | bytes 516104 | tf_op jit(solution)/shard_map/cond/branch_6_fun/ppermute | solution.py:477
  6.6 7.7 %collective-permute-start.37 = (f32[336,128]{1,0:T(8,128)S(1)}, f32[336,128]{1,0:T(8,128)S(1)}, u32[]{:S(2)}, u32[]{:S(2)}) collective-permute-start(f32[336,128]{1,0:T(8,128)S(1)} %get-tuple-element.202), channel_id=1, source_target_pairs={{0,4},{8,12},{16,20},{24,28},{1,5},{9,13},{17,21},{25,29},{2,6},{1... | collective-permute-start | bytes 516104 | tf_op jit(solution)/shard_map/cond/branch_6_fun/ppermute | solution.py:477
  6.6 6.1 %collective-permute-start.39 = (f32[7,3,8,128]{3,2,1,0:T(8,128)S(1)}, f32[7,3,8,128]{3,2,1,0:T(8,128)S(1)}, u32[]{:S(2)}, u32[]{:S(2)}) collective-permute-start(f32[7,3,8,128]{3,2,1,0:T(8,128)S(1)} %get-tuple-element.205), channel_id=1, source_target_pairs={{1,0},{5,4},{9,8},{13,12},{17,16},{21,20},{25,24},{29,28},{2,1},{6... | collective-permute-start | bytes 258056 | tf_op jit(solution)/shard_map/cond/branch_6_fun/ppermute | solution.py:477
  12.8 5.2 %collective-permute-start.40 = (f32[160,128]{1,0:T(8,128)S(1)}, f32[160,128]{1,0:T(8,128)S(1)}, u32[]{:S(2)}, u32[]{:S(2)}) collective-permute-start(f32[160,128]{1,0:T(8,128)S(1)} %get-tuple-element.207), channel_id=1, source_target_pairs={{4,8},{12,16},{20,24},{28,0},{5,9},{13,17},{21,25},{29,1},{6,10},{... | collective-permute-start | bytes 245768 | tf_op jit(solution)/shard_map/cond/branch_6_fun/ppermute | solution.py:477
  13.4 4.5 %collective-permute-start.41 = (f32[160,128]{1,0:T(8,128)S(1)}, f32[160,128]{1,0:T(8,128)S(1)}, u32[]{:S(2)}, u32[]{:S(2)}) collective-permute-start(f32[160,128]{1,0:T(8,128)S(1)} %get-tuple-element.208), channel_id=1, source_target_pairs={{0,4},{8,12},{16,20},{24,28},{1,5},{9,13},{17,21},{25,29},{2,6},{1... | collective-permute-start | bytes 245768 | tf_op jit(solution)/shard_map/cond/branch_6_fun/ppermute | solution.py:477
  14.3 1.0 %copy-start.7 = (f32[7,16,8,128]{3,2,1,0:T(8,128)S(1)}, f32[7,16,8,128]{3,2,1,0:T(8,128)}, u32[]{:S(2)}) copy-start(f32[7,16,8,128]{3,2,1,0:T(8,128)} %get-tuple-element.298.register) | copy-start | bytes 1376260 | tf_op jit(solution)/shard_map/cond
where the time goes:
time: 20.2 us; the launch traced here: 20 us
  starting transfers between devices  9.82 us (49%)
  Pallas kernels  4.84 us (24%)
  waiting for transfers between devices  3.07 us (15%)
  between operations  1.59 us (8%)
  loops' own time  0.39 us (2%)
  local copies, waits for them, and re-layouts  0.25 us (1%)
    ppermute x6, starting transfers between devices, send(): return lax.ppermute(value, ('yz', 'gx'), pairs)  9.82 us
    ppermute x6, waiting for transfers between devices, send(): return lax.ppermute(value, ('yz', 'gx'), pairs)  3.07 us
    pallas_call x1, Pallas kernels, exchange(): pl.pallas_call(functools.partial(edge_kernel, cells_x, slabs_x, 1.0 / tot...  1.55 us
    pallas_call x1, Pallas kernels, exchange(): pl.pallas_call(functools.partial(side_kernel, cells_x), out_shape=shape(1...  0.99 us
    pallas_call x1, Pallas kernels, exchange(): pl.pallas_call(functools.partial(own_z_kernel, cells_x), out_shape=[shape...  0.94 us
    pallas_call x1, Pallas kernels, exchange(): pl.pallas_call(functools.partial(inner_kernel, cells_x, 1.0 / total_x), o...  0.92 us
  transfers between devices with their start and end apart: 6, of which 3 were waited for; matrix products, arithmetic and copies ran while one was open for 0% of the time, Pallas kernels for 16%

commit v1 on v0

--- a/solution.py
+++ b/solution.py
@@ -15,7 +15,7 @@
 DEEP = (0, 2, 3, 5)
 SHEAR_Z = (1, 2, 4, 5)
 ROW = 8
-LOW = 10**9
+NEAR = 6 * 10**8
 EARLY = 4
 TALL = 24
 VMEM = 32 * 1024 * 1024
@@ -135,8 +135,8 @@
     down[...] = state[:, :3]
 
 
-def low_kernel(x_low, after, low):
-    low[...] = x_low[...]
+def keep_kernel(received, after, kept):
+    kept[...] = received[...]
 
 
 def row_kernel(cells_x, cells_y, state, y_near, y_far):
@@ -246,11 +246,16 @@
     lax.fori_loop(0, (end - begin) // 2, two, 0)
 
 
-def corner_kernel(slabs_x, low, x_high, faces, far, near):
+def corner_kernel(slabs_x, low, high, wrapped, faces, far, near):
     where_x = lax.axis_index("gx")
     y_odd = lax.axis_index("yz") % 2
     faces[0] = low[...]
-    faces[1] = x_high[...]
+
+    def take(source):
+        faces[1] = source[...]
+
+    pl.when(where_x != slabs_x - 1)(functools.partial(take, high))
+    pl.when(where_x == slabs_x - 1)(functools.partial(take, wrapped))
 
     def fill(to_next, to_last):
         for side in range(2):
@@ -488,9 +493,11 @@
         pairs = [(place(slab, j), place(slab + 1, j)) for slab in range(last) for j in range(slabs_y)]
         return pairs + [(place(last, j + by), place(0, j)) for j in range(slabs_y)]
 
-    def downward(by):
-        pairs = [(place(slab + 1, j), place(slab, j)) for slab in range(last) for j in range(slabs_y)]
-        return pairs + [(place(0, j - by), place(last, j)) for j in range(slabs_y)]
+    def downward():
+        return [(place(slab + 1, j), place(slab, j)) for slab in range(last) for j in range(slabs_y)]
+
+    def around(by):
+        return [(place(0, j - by), place(last, j)) for j in range(slabs_y)]
 
     last = slabs_x - 1
 
@@ -539,8 +546,8 @@
         plane = state.shape[1:]
         if up is None:
             up, down = faces_of(state)
+        x_high = send(down, downward())
         x_low = send(up, upward(by))
-        x_high = send(down, downward(by))
         y_near, y_far = pl.pallas_call(
             functools.partial(row_kernel, cells_x, cells_y),
             out_shape=[shape(21 * cells_x, LANES), shape(21 * cells_x, LANES)],
@@ -560,22 +567,28 @@
             compiler_params=params,
             cost_estimate=cost(10**8),
         )(state, weights, forcing)
-        low = pl.pallas_call(
-            low_kernel,
-            out_shape=shape(*up.shape),
-            in_specs=[vmem, anyspace],
-            out_specs=vmem,
-            compiler_params=params,
-            cost_estimate=cost(LOW, 1),
-        )(x_low, dz)
+
+        def keep(received, after):
+            return pl.pallas_call(
+                keep_kernel,
+                out_shape=shape(*up.shape),
+                in_specs=[vmem, anyspace],
+                out_specs=vmem,
+                compiler_params=params,
+                cost_estimate=cost(NEAR, 1),
+            )(received, after)
+
+        high = keep(x_high, dz)
+        low = keep(x_low, high)
+        wrapped = send(down, around(by))
         faces, far, near = pl.pallas_call(
             functools.partial(corner_kernel, slabs_x),
             out_shape=[shape(2, *up.shape), shape(160, LANES), shape(160, LANES)],
-            in_specs=[vmem] * 2,
+            in_specs=[vmem] * 3,
             out_specs=[vmem] * 3,
             compiler_params=params,
             cost_estimate=cost(1, 1),
-        )(low, x_high)
+        )(low, high, wrapped)
         far = send(far, y_pairs(1))
         near = send(near, y_pairs(0))
         x_parts = pl.pallas_call(

time: 20.2 us -> 22.7 us (1.12)
  starting transfers between devices: 9.82 us -> 13 us
  waiting for transfers between devices: 3.07 us -> 2.47 us
    ppermute x6 -> x7, starting transfers between devices: 9.82 us -> 13 us  [send(): return lax.ppermute(value, ('yz', 'gx'), pairs)]
    ppermute x6 -> x7, waiting for transfers between devices: 3.07 us -> 2.47 us  [send(): return lax.ppermute(value, ('yz', 'gx'), pairs)]
  transfers between devices with their start and end apart: 6 -> 7, of which waited for: 3 -> 2; matrix products, arithmetic and copies ran while one was open for 0% -> 0% of each run, Pallas kernels for 16% -> 14%
where the time goes in v1:
time: 22.7 us; the launch traced here: 22.6 us
  starting transfers between devices  13 us (57%)
  Pallas kernels  4.87 us (21%)
  waiting for transfers between devices  2.47 us (11%)
  between operations  1.59 us (7%)
  loops' own time  0.45 us (2%)
  local copies, waits for them, and re-layouts  0.23 us (1%)
    ppermute x7, starting transfers between devices, send(): return lax.ppermute(value, ('yz', 'gx'), pairs)  13 us
    ppermute x7, waiting for transfers between devices, send(): return lax.ppermute(value, ('yz', 'gx'), pairs)  2.47 us
    pallas_call x1, Pallas kernels, exchange(): pl.pallas_call(functools.partial(edge_kernel, cells_x, slabs_x, 1.0 / tot...  1.55 us
    pallas_call x1, Pallas kernels, exchange(): pl.pallas_call(functools.partial(side_kernel, cells_x), out_shape=shape(1...  1 us
    pallas_call x1, Pallas kernels, exchange(): pl.pallas_call(functools.partial(own_z_kernel, cells_x), out_shape=[shape...  0.94 us
    pallas_call x1, Pallas kernels, exchange(): pl.pallas_call(functools.partial(inner_kernel, cells_x, 1.0 / total_x), o...  0.93 us
    another operation x1, loops' own time, per_device(): lax.switch(steps % digit, [functools.partial(exchange, by) for by in rang...  0.45 us
  transfers between devices with their start and end apart: 7, of which 2 were waited for; matrix products, arithmetic and copies ran while one was open for 0% of the time, Pallas kernels for 14%

profile of v1, /device:TPU:0, one launch (start us, length us, event | category | flops | bytes accessed | tf_op | source)
XLA Modules:
  0.0 22.6 jit_solution(4755111741992649185)
XLA Ops:
  0.6 0.0 copy-start
  1.4 0.1 shard_map.99
  1.4 0.2 copy-done
  1.7 20.7 %conditional.1 = ((f32[7,16,8,128]{3,2,1,0:T(8,128)}, f32[7,16,8,128]{3,2,1,0:T(8,128)})) conditional(s32[]{:T(128)} %clamp.3, (f32[7,16,8,128]{3,2,1,0:T(8,128)S(1)}, bf16[256,256]{1,0:T(8,128)(2,1)S(1)}, f32[3,16,8,128]{3,2,1,0:T(8,128)}, f32[7,16,8,128]{3,2,1,0:T(8,128)}, s32[8,128]{1,0:T(8,128)S(1)}) %tuple.64, ...), branch_computations={%region_0.1_spmd, %region_1.2_spmd, %region_2.3_spmd, %region_3.4_... | conditional | flops 1700000000 | bytes 7899136 | solution.py:649
  1.7 1.3 %collective-permute-start.52 = (f32[7,3,8,128]{3,2,1,0:T(8,128)S(1)}, f32[7,3,8,128]{3,2,1,0:T(8,128)S(1)}, u32[]{:S(2)}, u32[]{:S(2)}) collective-permute-start(f32[7,3,8,128]{3,2,1,0:T(8,128)S(1)} %get-tuple-element.224), channel_id=1, source_target_pairs={{1,0},{5,4},{9,8},{13,12},{17,16},{21,20},{25,24},{29,28},{2,1},{6... | collective-permute-start | bytes 258056 | tf_op jit(solution)/shard_map/cond/branch_7_fun/ppermute | solution.py:482
  3.0 3.7 %collective-permute-start.51 = (f32[7,3,8,128]{3,2,1,0:T(8,128)S(1)}, f32[7,3,8,128]{3,2,1,0:T(8,128)S(1)}, u32[]{:S(2)}, u32[]{:S(2)}) collective-permute-start(f32[7,3,8,128]{3,2,1,0:T(8,128)S(1)} %get-tuple-element.223), channel_id=1, source_target_pairs={{0,1},{4,5},{8,9},{12,13},{16,17},{20,21},{24,25},{28,29},{1,2},{5... | collective-permute-start | bytes 258056 | tf_op jit(solution)/shard_map/cond/branch_7_fun/ppermute | solution.py:482
  6.8 0.1 branch_7_fun.11
  6.8 1.8 %collective-permute-start.49 = (f32[336,128]{1,0:T(8,128)S(1)}, f32[336,128]{1,0:T(8,128)S(1)}, u32[]{:S(2)}, u32[]{:S(2)}) collective-permute-start(f32[336,128]{1,0:T(8,128)S(1)} %get-tuple-element.220), channel_id=1, source_target_pairs={{4,8},{12,16},{20,24},{28,0},{5,9},{13,17},{21,25},{29,1},{6,10},{... | collective-permute-start | bytes 516104 | tf_op jit(solution)/shard_map/cond/branch_7_fun/ppermute | solution.py:482
  8.7 0.3 %collective-permute-start.50 = (f32[336,128]{1,0:T(8,128)S(1)}, f32[336,128]{1,0:T(8,128)S(1)}, u32[]{:S(2)}, u32[]{:S(2)}) collective-permute-start(f32[336,128]{1,0:T(8,128)S(1)} %get-tuple-element.221), channel_id=1, source_target_pairs={{0,4},{8,12},{16,20},{24,28},{1,5},{9,13},{17,21},{25,29},{2,6},{1... | collective-permute-start | bytes 516104 | tf_op jit(solution)/shard_map/cond/branch_7_fun/ppermute | solution.py:482
  9.0 4.6 %collective-permute-start.53 = (f32[7,3,8,128]{3,2,1,0:T(8,128)S(1)}, f32[7,3,8,128]{3,2,1,0:T(8,128)S(1)}, u32[]{:S(2)}, u32[]{:S(2)}) collective-permute-start(f32[7,3,8,128]{3,2,1,0:T(8,128)S(1)} %get-tuple-element.224), channel_id=1, source_target_pairs={{4,3},{8,7},{12,11},{16,15},{20,19},{24,23},{28,27},{0,31}} | collective-permute-start | bytes 258056 | tf_op jit(solution)/shard_map/cond/branch_7_fun/ppermute | solution.py:482
  13.6 0.9 %branch_7_fun.10 = (f32[7,16,8,128]{3,2,1,0:T(8,128)S(1)}, f32[5,16,8,128]{3,2,1,0:T(8,128)S(1)}, f32[3,16,8,128]{3,2,1,0:T(8,128)S(1)}) custom-call(f32[7,16,8,128]{3,2,1,0:T(8,128)S(1)} %get-tuple-element.283.state, bf16[256,256]{1,0:T(8,128)(2,1)S(1)} %get-tuple-element.216.weights, f32[3,16,8,128]{3,2,1,0:T(8,128)} %get-tuple-element.291.forcing), custom_call_target="tpu_custom_call" | custom-call | flops 100000000 | bytes 1000000 | tf_op jit(solution)/shard_map/cond/branch_7_fun/pallas_call | solution.py:561
  14.6 0.0 collective-permute-done.52.received
  14.6 0.0 collective-permute-done.51.received
  14.6 1.1 %collective-permute-done.53.wrapped = f32[7,3,8,128]{3,2,1,0:T(8,128)S(1)} collective-permute-done((f32[7,3,8,128]{3,2,1,0:T(8,128)S(1)}, f32[7,3,8,128]{3,2,1,0:T(8,128)S(1)}, u32[]{:S(2)}, u32[]{:S(2)}) %collective-permute-start.53) | collective-permute-done | bytes 86048 | tf_op jit(solution)/shard_map/cond/branch_7_fun/ppermute | solution.py:482
  15.7 0.1 branch_7_fun.15
  15.8 0.1 collective-permute-start.54
  15.8 1.2 %collective-permute-start.55 = (f32[160,128]{1,0:T(8,128)S(1)}, f32[160,128]{1,0:T(8,128)S(1)}, u32[]{:S(2)}, u32[]{:S(2)}) collective-permute-start(f32[160,128]{1,0:T(8,128)S(1)} %get-tuple-element.227), channel_id=1, source_target_pairs={{0,4},{8,12},{16,20},{24,28},{1,5},{9,13},{17,21},{25,29},{2,6},{1... | collective-permute-start | bytes 245768 | tf_op jit(solution)/shard_map/cond/branch_7_fun/ppermute | solution.py:482
  17.0 0.2 %branch_7_fun.16.after.x_parts = f32[13,10,8,128]{3,2,1,0:T(8,128)S(1)} custom-call(f32[7,16,8,128]{3,2,1,0:T(8,128)S(1)} %get-tuple-element.283.state, f32[7,16,8,128]{3,2,1,0:T(8,128)S(1)} %get-tuple-element.219.after.dz, f32[2,7,3,8,128]{4,3,2,1,0:T(8,128)S(1)} %get-tuple-element.225.after.planes), custom_call_target="tpu_custom_call" | custom-call | flops 1 | bytes 1 | tf_op jit(solution)/shard_map/cond/branch_7_fun/pallas_call | solution.py:594
  17.2 0.0 collective-permute-done.49.y_far
  17.2 0.0 collective-permute-done.50.y_near
  17.2 0.0 copy-start.8
  17.2 1.0 %branch_7_fun.17.side_terms = f32[13,16,8,128]{3,2,1,0:T(8,128)S(1)} custom-call(f32[7,16,8,128]{3,2,1,0:T(8,128)S(1)} %get-tuple-element.283.state, bf16[256,256]{1,0:T(8,128)(2,1)S(1)} %get-tuple-element.216.weights, f32[336,128]{1,0:T(8,128)S(1)} %collective-permute-done.49.y_far, f32[336,128]{1,0:T(8,128)S(1)} %collective-permute-done.50.y_near, ...), custom_call_target="tpu_custom_call" | custom-call | flops 200000000 | bytes 1000000 | tf_op jit(solution)/shard_map/cond/branch_7_fun/pallas_call | solution.py:602
  18.2 0.0 copy-done.8
  18.3 0.9 %branch_7_fun.18 = (f32[7,16,8,128]{3,2,1,0:T(8,128)}, f32[7,16,8,128]{3,2,1,0:T(8,128)}, f32[7,6,8,128]{3,2,1,0:T(8,128)S(1)}, f32[7,6,8,128]{3,2,1,0:T(8,128)S(1)}) custom-call(f32[7,16,8,128]{3,2,1,0:T(8,128)S(1)} %get-tuple-element.283.state, f32[7,16,8,128]{3,2,1,0:T(8,128)S(1)} %copy-done.8, f32[3,16,8,128]{3,2,1,0:T(8,128)S(1)} %get-tuple-element.218.forcing, ...), custom_call_target="tpu_custom_call" | custom-call | flops 200000000 | bytes 1000000 | tf_op jit(solution)/shard_map/cond/branch_7_fun/pallas_call | solution.py:615
  19.2 1.4 %collective-permute-done.54.far = f32[160,128]{1,0:T(8,128)S(1)} collective-permute-done((f32[160,128]{1,0:T(8,128)S(1)}, f32[160,128]{1,0:T(8,128)S(1)}, u32[]{:S(2)}, u32[]{:S(2)}) %collective-permute-start.54) | collective-permute-done | bytes 81952 | tf_op jit(solution)/shard_map/cond/branch_7_fun/ppermute | solution.py:482
  20.6 0.0 collective-permute-done.55.near
  20.6 1.6 %branch_7_fun.19 = (f32[7,16,8,128]{3,2,1,0:T(8,128)}, f32[7,16,8,128]{3,2,1,0:T(8,128)}) custom-call(s32[8,128]{1,0:T(8,128)S(1)} %get-tuple-element.213.lean_tile, f32[7,16,8,128]{3,2,1,0:T(8,128)S(1)} %get-tuple-element.283.state, f32[7,16,8,128]{3,2,1,0:T(8,128)S(1)} %copy-done.8, ...), custom_call_target="tpu_custom_call", output_to_operand_aliasing={{0}: (12, {}), {1}: (13, {})} | custom-call | tf_op jit(solution)/shard_map/cond/branch_7_fun/pallas_call | solution.py:628
  (4 shorter events, 0.0 us)
Async XLA Ops:
  0.6 1.0 %copy-start = (f32[7,16,8,128]{3,2,1,0:T(8,128)S(1)}, f32[7,16,8,128]{3,2,1,0:T(8,128)}, u32[]{:S(2)}) copy-start(f32[7,16,8,128]{3,2,1,0:T(8,128)} %param.12) | copy-start | bytes 1376260
  1.7 12.8 %collective-permute-start.52 = (f32[7,3,8,128]{3,2,1,0:T(8,128)S(1)}, f32[7,3,8,128]{3,2,1,0:T(8,128)S(1)}, u32[]{:S(2)}, u32[]{:S(2)}) collective-permute-start(f32[7,3,8,128]{3,2,1,0:T(8,128)S(1)} %get-tuple-element.224), channel_id=1, source_target_pairs={{1,0},{5,4},{9,8},{13,12},{17,16},{21,20},{25,24},{29,28},{2,1},{6... | collective-permute-start | bytes 258056 | tf_op jit(solution)/shard_map/cond/branch_7_fun/ppermute | solution.py:482
  3.0 11.5 %collective-permute-start.51 = (f32[7,3,8,128]{3,2,1,0:T(8,128)S(1)}, f32[7,3,8,128]{3,2,1,0:T(8,128)S(1)}, u32[]{:S(2)}, u32[]{:S(2)}) collective-permute-start(f32[7,3,8,128]{3,2,1,0:T(8,128)S(1)} %get-tuple-element.223), channel_id=1, source_target_pairs={{0,1},{4,5},{8,9},{12,13},{16,17},{20,21},{24,25},{28,29},{1,2},{5... | collective-permute-start | bytes 258056 | tf_op jit(solution)/shard_map/cond/branch_7_fun/ppermute | solution.py:482
  6.8 10.4 %collective-permute-start.49 = (f32[336,128]{1,0:T(8,128)S(1)}, f32[336,128]{1,0:T(8,128)S(1)}, u32[]{:S(2)}, u32[]{:S(2)}) collective-permute-start(f32[336,128]{1,0:T(8,128)S(1)} %get-tuple-element.220), channel_id=1, source_target_pairs={{4,8},{12,16},{20,24},{28,0},{5,9},{13,17},{21,25},{29,1},{6,10},{... | collective-permute-start | bytes 516104 | tf_op jit(solution)/shard_map/cond/branch_7_fun/ppermute | solution.py:482
  8.7 8.6 %collective-permute-start.50 = (f32[336,128]{1,0:T(8,128)S(1)}, f32[336,128]{1,0:T(8,128)S(1)}, u32[]{:S(2)}, u32[]{:S(2)}) collective-permute-start(f32[336,128]{1,0:T(8,128)S(1)} %get-tuple-element.221), channel_id=1, source_target_pairs={{0,4},{8,12},{16,20},{24,28},{1,5},{9,13},{17,21},{25,29},{2,6},{1... | collective-permute-start | bytes 516104 | tf_op jit(solution)/shard_map/cond/branch_7_fun/ppermute | solution.py:482
  9.0 6.7 %collective-permute-start.53 = (f32[7,3,8,128]{3,2,1,0:T(8,128)S(1)}, f32[7,3,8,128]{3,2,1,0:T(8,128)S(1)}, u32[]{:S(2)}, u32[]{:S(2)}) collective-permute-start(f32[7,3,8,128]{3,2,1,0:T(8,128)S(1)} %get-tuple-element.224), channel_id=1, source_target_pairs={{4,3},{8,7},{12,11},{16,15},{20,19},{24,23},{28,27},{0,31}} | collective-permute-start | bytes 258056 | tf_op jit(solution)/shard_map/cond/branch_7_fun/ppermute | solution.py:482
  15.8 4.8 %collective-permute-start.54 = (f32[160,128]{1,0:T(8,128)S(1)}, f32[160,128]{1,0:T(8,128)S(1)}, u32[]{:S(2)}, u32[]{:S(2)}) collective-permute-start(f32[160,128]{1,0:T(8,128)S(1)} %get-tuple-element.226), channel_id=1, source_target_pairs={{4,8},{12,16},{20,24},{28,0},{5,9},{13,17},{21,25},{29,1},{6,10},{... | collective-permute-start | bytes 245768 | tf_op jit(solution)/shard_map/cond/branch_7_fun/ppermute | solution.py:482
  15.8 4.8 %collective-permute-start.55 = (f32[160,128]{1,0:T(8,128)S(1)}, f32[160,128]{1,0:T(8,128)S(1)}, u32[]{:S(2)}, u32[]{:S(2)}) collective-permute-start(f32[160,128]{1,0:T(8,128)S(1)} %get-tuple-element.227), channel_id=1, source_target_pairs={{0,4},{8,12},{16,20},{24,28},{1,5},{9,13},{17,21},{25,29},{2,6},{1... | collective-permute-start | bytes 245768 | tf_op jit(solution)/shard_map/cond/branch_7_fun/ppermute | solution.py:482
  17.2 1.0 %copy-start.8 = (f32[7,16,8,128]{3,2,1,0:T(8,128)S(1)}, f32[7,16,8,128]{3,2,1,0:T(8,128)}, u32[]{:S(2)}) copy-start(f32[7,16,8,128]{3,2,1,0:T(8,128)} %get-tuple-element.299.register) | copy-start | bytes 1376260 | tf_op jit(solution)/shard_map/cond
